TPU v7x, 32 devices: a whole 2x2x4 slice. The times are simulated.
32 devices in a mesh: mem: 4 (over y, x), lon: 8 (over z, core).
Axes of the slice: x: 2, y: 2, z: 4, core: 2. Of those that a mesh axis runs over, the one named last changes fastest.
Arguments:
- members: float32 [16, 256, 12, 720], P('mem', 'lon'), may hold values from -6 to 6
- control: float32 [256, 12, 720], P('lon', None, 'mem'), may hold values from -6 to 6
- sea_mask: int32 [256, 12], P('lon'), may hold values 0 or 1
- depth_class: int32 [256, 12], P('lon'), may hold values from 0 to 3
- wind_dir: int32 [256, 12], P('lon'), may hold values from 0 to 23
- growth: float32 [30], replicated, may hold values from 0.2 to 2
- kernel: float32 [720, 720], replicated, may hold values from -0.21875 to 0.21875
Outputs:
- spectra: float32 [16, 256, 12, 720], P('mem', 'lon')
All inputs are finite; a program needn't handle non-finite values. No bound on the sum of `sea_mask` on one device may be relied on, other than what follows from the above.
Results may differ from a plain program's by a relative error of at most 0.0001.
Values sent between devices are 32-bit elements; how exact they have to be, the bound alone decides.
A program may use at most 128 MiB of HBM per device.

v0:
```python
import math
import jax
import jax.numpy as jnp
from jax import lax
from jax.sharding import PartitionSpec as P

DIRS = 24
FREQS = 30


def extended(x, sides, width):
    for axis, dim in sides:
        count, length = (lax.axis_size(axis), x.shape[dim])
        up = [(i, (i + 1) % count) for i in range(count)]
        down = [(j, i) for i, j in up]
        last = lax.slice_in_dim(x, length - width, length, axis=dim)
        initial = lax.slice_in_dim(x, 0, width, axis=dim)
        before = lax.ppermute(last, axis, up)
        after = lax.ppermute(initial, axis, down)
        x = jnp.concatenate([before, x, after], axis=dim)
    return x


def wave_tables(sea_mask, depth_class, wind_dir, growth):
    cells_lon, rows_lat = sea_mask.shape
    frequency = 0.04 * jnp.power(jnp.float32(1.1), jnp.arange(FREQS).astype(jnp.float32))
    deep_speed = 9.81 / (4.0 * math.pi * frequency)
    depths = jnp.array([10.0, 30.0, 80.0, 200.0], jnp.float32)
    shallow = jnp.sqrt(9.81 * depths)
    group_speed = jnp.minimum(deep_speed[None, :], shallow[:, None])
    fastest = 9.81 / (4.0 * math.pi * 0.04)
    onehot = (depth_class[..., None] == jnp.arange(4)).astype(jnp.float32)
    cell_speed = 0.7 * jnp.sum(onehot[..., None] * group_speed, axis=2) / fastest
    angles = 2.0 * math.pi * jnp.arange(DIRS).astype(jnp.float32) / DIRS
    zonal_speed = (cell_speed[:, :, None, :] * jnp.cos(angles)[:, None]).reshape(
        cells_lon, rows_lat, DIRS * FREQS
    )
    merid_speed = (cell_speed[:, :, None, :] * jnp.sin(angles)[:, None]).reshape(
        cells_lon, rows_lat, DIRS * FREQS
    )
    relative = (jnp.arange(DIRS)[None, None, :] - wind_dir[..., None]).astype(jnp.float32)
    alignment = jnp.maximum(jnp.cos(2.0 * math.pi * relative / DIRS), 0.0)
    wind_gain = (alignment[..., None] * growth[None, None, None, :]).reshape(
        cells_lon, rows_lat, DIRS * FREQS
    )
    ocean = sea_mask.astype(jnp.float32)[..., None]
    return (zonal_speed, merid_speed, wind_gain, ocean)


def advect(centre, west_side, east_side, zonal_speed, merid_speed):
    lat_pad = jnp.pad(centre, ((0, 0), (0, 0), (1, 1), (0, 0)))
    south_side = lat_pad[:, :, :-2]
    north_side = lat_pad[:, :, 2:]
    flux = jnp.maximum(zonal_speed, 0.0) * (centre - west_side) + jnp.minimum(zonal_speed, 0.0) * (
        east_side - centre
    )
    flux = (
        flux
        + jnp.maximum(merid_speed, 0.0) * (centre - south_side)
        + jnp.minimum(merid_speed, 0.0) * (north_side - centre)
    )
    return centre - flux


def source(field, wind_gain, ocean, kernel):
    energy = jnp.mean(field * field, axis=-1, keepdims=True)
    shape = field.shape
    transfer = jnp.dot(
        field.reshape(-1, shape[-1]),
        kernel,
        precision=lax.Precision.HIGHEST,
        preferred_element_type=jnp.float32,
    ).reshape(shape)
    return (field + 0.1 * (wind_gain * field - 0.5 * energy * field + transfer)) * ocean


def padded_step(padded, tables, kernel):
    zonal_speed, merid_speed, wind_gain, ocean = tables
    moved = advect(padded[:, 1:-1], padded[:, :-2], padded[:, 2:], zonal_speed, merid_speed)
    return source(moved, wind_gain, ocean, kernel)


def thin_step(field, tables, kernel):
    padded = extended(field, (("lon", 1),), 1)
    return padded_step(padded, tables, kernel)


def shards(members, control, sea_mask, depth_class, wind_dir, growth, kernel):
    member_count = members.shape[0] * lax.axis_size("mem")
    local_total = jnp.sum(members, axis=0)
    tables = wave_tables(sea_mask, depth_class, wind_dir, growth)
    ocean = tables[3]
    member_total = lax.psum(local_total, "mem")
    control_full = lax.all_gather(control, "mem", axis=2, tiled=True)
    field = (members - member_total / member_count + control_full) * ocean
    field = thin_step(field, tables, kernel)
    field = thin_step(field, tables, kernel)
    return field


def solution(mesh):
    return jax.shard_map(
        shards,
        mesh=mesh,
        in_specs=(
            P("mem", "lon", None, None),
            P("lon", None, "mem"),
            P("lon", None),
            P("lon", None),
            P("lon", None),
            P(),
            P(),
        ),
        out_specs=P("mem", "lon", None, None),
        check_vma=False,
    )
```

profile of v0, /device:TPU:0, one launch (start us, length us, event | category | flops | bytes accessed | tf_op | source)
XLA Modules:
  0.0 206.2 jit_solution(917678572837277976)
XLA Ops:
  6.5 0.0 copy-start
  6.5 0.0 copy-start.8
  6.6 0.0 copy-start.6
  6.6 0.0 all-reduce.4.cloned.1.call-start
  6.6 4.0 %reduce_sum.36 = f32[32,12,720]{2,0,1:T(8,128)} reduce(f32[4,32,12,720]{3,1,2,0:T(8,128)} %param.8, f32[]{:T(128)} %constant.14.clone.1), dimensions={0}, to_apply=%region_0.0 | reduce | flops 829440 | bytes 5529604 | tf_op jit(solution)/shard_map/reduce_sum | solution.py:90
  10.6 0.0 all-reduce.4.cloned.1.call-update
  10.7 0.0 all-gather.2.cloned.1.call-start
  10.7 0.0 copy-done.5
  10.7 2.0 copy.14
  12.7 0.0 all-gather.2.cloned.1.call-update
  12.8 0.0 copy-done.7
  12.8 0.1 mul.260
  12.9 0.1 mul.261
  13.0 0.1 mul.252
  13.1 0.1 mul.253
  13.2 0.0 copy-done.9
  13.2 0.1 mul.271
  13.3 0.0 copy-done.10
  13.3 0.1 broadcast_minimum_fusion
  13.4 0.5 multiply_reduce_fusion.2
  14.0 0.1 copy.16
  14.1 0.7 cosine_maximum_fusion
  14.8 3.2 %mul.268 = f32[32,12,24,30]{3,2,0,1:T(8,128)} broadcast(f32[32,12,24]{2,0,1:T(8,128)S(1)} %cosine_maximum_fusion), dimensions={0,1,2} | broadcast | bytes 1142784 | tf_op jit(solution)/shard_map/mul | solution.py:43
  18.1 4.9 %mul.269 = f32[32,12,720]{2,0,1:T(8,128)} reshape(f32[32,12,24,30]{3,2,0,1:T(8,128)} %mul.268) | data formatting | bytes 2211840 | tf_op jit(solution)/shard_map/mul | solution.py:43
  22.9 2.5 %mul.250 = f32[32,12,24,30]{3,2,0,1:T(8,128)} broadcast(f32[32,12,30]{2,0,1:T(8,128)S(1)} %copy.16), dimensions={0,1,3} | broadcast | bytes 1152000 | tf_op jit(solution)/shard_map/mul | solution.py:35
  25.4 4.6 %mul.251 = f32[32,12,720]{2,0,1:T(8,128)} reshape(f32[32,12,24,30]{3,2,0,1:T(8,128)} %mul.250) | data formatting | bytes 2211840 | tf_op jit(solution)/shard_map/mul | solution.py:35
  30.0 3.3 %multiply_maximum_fusion.1 = (f32[32,12,720]{2,0,1:T(8,128)S(1)}, f32[32,12,720]{2,0,1:T(8,128)}, f32[32,12,720]{2,0,1:T(8,128)}, f32[32,12,720]{2,0,1:T(8,128)}) fusion(f32[32,12,720]{2,0,1:T(8,128)} %mul.251, f32[720]{0:T(1024)S(1)} %mul.253, f32[720]{0:T(1024)S(1)} %mul.261), kind=kLoop, calls=%fused_computation.44 | loop fusion | flops 1658880 | bytes 5535360 | tf_op jit(solution)/shard_map/max | solution.py:54
  33.3 34.7 %all-reduce.4.cloned.1.call-done = f32[32,12,720]{2,0,1:T(8,128)} async-done(((f32[32,12,720]{2,0,1:T(8,128)}), f32[32,12,720]{2,0,1:T(8,128)}) %all-reduce.4.cloned.1.call-update) | async-done | bytes 1105936 | tf_op jit(solution)/shard_map/psum | solution.py:93
  68.0 2.4 %broadcast_multiply_fusion.1 = f32[32,12,720]{2,0,1:T(8,128)} fusion(f32[32,12,720]{2,0,1:T(8,128)} %all-reduce.4.cloned.1.call-done), kind=kLoop, calls=%fused_computation.47 | loop fusion | flops 276480 | bytes 2211840 | tf_op jit(solution)/shard_map/div | solution.py:95
  70.4 66.5 %all-gather.2.cloned.1.call-done = f32[32,12,720]{0,1,2:T(8,128)} async-done(((f32[32,12,180]{0,1,2:T(8,128)}), f32[32,12,720]{0,1,2:T(8,128)}) %all-gather.2.cloned.1.call-update) | async-done | bytes 1105936 | tf_op jit(solution)/shard_map/all_gather | solution.py:94
  136.9 5.4 %copy.15 = f32[32,12,720]{2,0,1:T(8,128)} copy(f32[32,12,720]{0,1,2:T(8,128)} %all-gather.2.cloned.1.call-done) | data formatting | bytes 2211840 | tf_op jit(solution)/shard_map/all_gather | solution.py:94
  142.3 4.1 %add_multiply_fusion.2 = f32[4,32,12,720]{3,1,2,0:T(8,128)S(1)} fusion(f32[4,32,12,720]{3,1,2,0:T(8,128)} %param.8, f32[32,12]{0,1:T(8,128)S(1)} %convert_element_type.39, f32[32,12,720]{2,0,1:T(8,128)} %copy.15, f32[32,12,720]{2,0,1:T(8,128)} %broadcast_multiply_fusion.1), kind=kLoop, calls=%fused_computation.36 | loop fusion | flops 3317760 | bytes 11060736 | tf_op jit(solution)/shard_map/mul | solution.py:95
  146.4 0.2 fusion.38
  146.6 0.1 collective-permute-start
  146.6 3.5 %collective-permute-start.1 = (f32[4,1,12,720]{3,1,2,0:T(1,128)S(1)}, f32[4,1,12,720]{3,1,2,0:T(1,128)S(1)}, u32[]{:S(2)}, u32[]{:S(2)}) collective-permute-start(f32[4,1,12,720]{3,1,2,0:T(1,128)S(1)} %get-tuple-element.12), channel_id=1, source_target_pairs={{1,0},{2,1},{3,2},{4,3},{5,4},{6,5},{7,6},{0,7},{9,8},{10,9},{11,1... | collective-permute-start | bytes 414728 | tf_op jit(solution)/shard_map/ppermute | solution.py:19
  150.2 0.1 broadcast_multiply_fusion
  150.3 2.9 %collective-permute-done = f32[4,1,12,720]{3,1,2,0:T(1,128)S(1)} collective-permute-done((f32[4,1,12,720]{3,1,2,0:T(1,128)S(1)}, f32[4,1,12,720]{3,1,2,0:T(1,128)S(1)}, u32[]{:S(2)}, u32[]{:S(2)}) %collective-permute-start) | collective-permute-done | bytes 138272 | tf_op jit(solution)/shard_map/ppermute | solution.py:18
  153.1 0.0 collective-permute-done.1
  153.1 0.0 copy-done.2
  153.2 4.5 %multiply_reduce_fusion.1 = (f32[4,32,12]{1,2,0:T(8,128)S(1)}, f32[4,32,12,720]{3,1,2,0:T(8,128)S(1)}) fusion(f32[4,32,12,720]{3,1,2,0:T(8,128)S(1)} %add_multiply_fusion.2, f32[32,12,720]{2,0,1:T(8,128)S(1)} %copy-done.2, f32[32,12,720]{2,0,1:T(8,128)S(1)} %copy-done.3, f32[4,1,12,720]{3,1,2,0:T(1,128)S(1)} %collective-permute-done.1, ...), kind=kLoop, calls=%fused_computation.35 | loop fusion | flops 17693184 | bytes 13553664 | tf_op jit(solution)/shard_map/reduce_sum | solution.py:66
  157.7 14.8 %add_multiply_fusion.1 = f32[4,32,12,720]{3,1,2,0:T(8,128)S(1)} fusion(f32[4,32,12,720]{3,1,2,0:T(8,128)S(1)} %get-tuple-element.8, f32[4,32,12]{1,2,0:T(8,128)S(1)} %broadcast_multiply_fusion.4, f32[32,12,720]{2,0,1:T(8,128)S(1)} %broadcast_multiply_fusion, f32[32,12]{0,1:T(8,128)S(1)} %convert_element_type.39, f32[720,720]{1,0:T(8,128)S(1)} %copy-done), kind=kOutput, calls=%fused_computation.34 | convolution fusion | flops 9562890240 | bytes 12034560 | tf_op jit(solution)/shard_map/dot_general | solution.py:68
  172.5 0.2 fusion.37
  172.7 1.3 collective-permute-start.2
  174.0 2.3 %collective-permute-start.3 = (f32[4,1,12,720]{3,1,2,0:T(1,128)S(1)}, f32[4,1,12,720]{3,1,2,0:T(1,128)S(1)}, u32[]{:S(2)}, u32[]{:S(2)}) collective-permute-start(f32[4,1,12,720]{3,1,2,0:T(1,128)S(1)} %get-tuple-element.10), channel_id=1, source_target_pairs={{1,0},{2,1},{3,2},{4,3},{5,4},{6,5},{7,6},{0,7},{9,8},{10,9},{11,1... | collective-permute-start | bytes 414728 | tf_op jit(solution)/shard_map/ppermute | solution.py:19
  176.3 4.0 %collective-permute-done.2 = f32[4,1,12,720]{3,1,2,0:T(1,128)S(1)} collective-permute-done((f32[4,1,12,720]{3,1,2,0:T(1,128)S(1)}, f32[4,1,12,720]{3,1,2,0:T(1,128)S(1)}, u32[]{:S(2)}, u32[]{:S(2)}) %collective-permute-start.2) | collective-permute-done | bytes 138272 | tf_op jit(solution)/shard_map/ppermute | solution.py:18
  180.3 0.0 collective-permute-done.3
  180.3 4.3 %multiply_reduce_fusion = (f32[4,32,12]{1,2,0:T(8,128)S(1)}, f32[4,32,12,720]{3,1,2,0:T(8,128)S(1)}) fusion(f32[4,32,12,720]{3,1,2,0:T(8,128)S(1)} %add_multiply_fusion.1, f32[32,12,720]{2,0,1:T(8,128)S(1)} %copy-done.2, f32[32,12,720]{2,0,1:T(8,128)S(1)} %copy-done.3, f32[4,1,12,720]{3,1,2,0:T(1,128)S(1)} %collective-permute-done.3, ...), kind=kLoop, calls=%fused_computation.33 | loop fusion | flops 17693184 | bytes 13553664 | tf_op jit(solution)/shard_map/reduce_sum | solution.py:66
  184.6 14.8 %add_multiply_fusion = f32[4,32,12,720]{3,1,2,0:T(8,128)} fusion(f32[4,32,12,720]{3,1,2,0:T(8,128)S(1)} %get-tuple-element.6, f32[4,32,12]{1,2,0:T(8,128)S(1)} %broadcast_multiply_fusion.3, f32[32,12,720]{2,0,1:T(8,128)S(1)} %broadcast_multiply_fusion, f32[32,12]{0,1:T(8,128)S(1)} %convert_element_type.39, f32[720,720]{1,0:T(8,128)S(1)} %copy-done), kind=kOutput, calls=%fused_computation.32 | convolution fusion | flops 9562890240 | bytes 12034560 | tf_op jit(solution)/shard_map/dot_general | solution.py:68
  (23 shorter events, 0.2 us)
Async XLA Ops:
  6.5 151.1 %copy-start = (f32[720,720]{1,0:T(8,128)S(1)}, f32[720,720]{1,0:T(8,128)}, u32[]{:S(2)}) copy-start(f32[720,720]{1,0:T(8,128)} %param.14) | copy-start | bytes 6220804
  6.5 6.7 %copy-start.10 = (f32[4]{0:T(128)S(1)}, f32[4]{0:T(128)}, u32[]{:S(2)}) copy-start(f32[4]{0:T(128)} %constant.49) | copy-start | bytes 52
  6.5 4.2 %copy-start.5 = (f32[32,12,180]{2,0,1:T(8,128)S(1)}, f32[32,12,180]{2,0,1:T(8,128)}, u32[]{:S(2)}) copy-start(f32[32,12,180]{2,0,1:T(8,128)} %param.9) | copy-start | bytes 829444
  6.5 6.3 %copy-start.7 = (s32[32,12]{0,1:T(8,128)S(1)}, s32[32,12]{0,1:T(8,128)}, u32[]{:S(2)}) copy-start(s32[32,12]{0,1:T(8,128)} %param.10) | copy-start | bytes 4612
  6.5 6.6 %copy-start.9 = (f32[30]{0:T(128)S(1)}, f32[30]{0:T(128)}, u32[]{:S(2)}) copy-start(f32[30]{0:T(128)} %param.13) | copy-start | bytes 364
  6.5 6.8 %copy-start.8 = (s32[32,12]{0,1:T(8,128)S(1)}, s32[32,12]{0,1:T(8,128)}, u32[]{:S(2)}) copy-start(s32[32,12]{0,1:T(8,128)} %param.11) | copy-start | bytes 4612
  6.6 7.6 %copy-start.6 = (s32[32,12]{0,1:T(8,128)S(1)}, s32[32,12]{0,1:T(8,128)}, u32[]{:S(2)}) copy-start(s32[32,12]{0,1:T(8,128)} %param.12) | copy-start | bytes 4612
  6.6 61.4 %all-reduce.4.cloned.1.call-start = ((), (), s32[]{:S(2)}) async-start(), calls=%async_computation | async-start | bytes 2359296 | tf_op jit(solution)/shard_map/psum | solution.py:93
  10.7 126.2 %all-gather.2.cloned.1.call-start = ((), (), s32[]{:S(2)}) async-start(), calls=%async_computation.1 | async-start | bytes 7372800 | tf_op jit(solution)/shard_map/all_gather | solution.py:94
  142.3 7.9 %copy-start.4 = (f32[32,12,720]{2,0,1:T(8,128)S(1)}, f32[32,12,720]{2,0,1:T(8,128)}, u32[]{:S(2)}) copy-start(f32[32,12,720]{2,0,1:T(8,128)} %mul.269) | copy-start | bytes 3317764
  142.3 10.9 %copy-start.1 = (f32[32,12,720]{2,0,1:T(8,128)S(1)}, f32[32,12,720]{2,0,1:T(8,128)}, u32[]{:S(2)}) copy-start(f32[32,12,720]{2,0,1:T(8,128)} %get-tuple-element.14) | copy-start | bytes 3317764
  142.3 10.9 %copy-start.2 = (f32[32,12,720]{2,0,1:T(8,128)S(1)}, f32[32,12,720]{2,0,1:T(8,128)}, u32[]{:S(2)}) copy-start(f32[32,12,720]{2,0,1:T(8,128)} %get-tuple-element.17) | copy-start | bytes 3317764
  142.3 10.9 %copy-start.3 = (f32[32,12,720]{2,0,1:T(8,128)S(1)}, f32[32,12,720]{2,0,1:T(8,128)}, u32[]{:S(2)}) copy-start(f32[32,12,720]{2,0,1:T(8,128)} %get-tuple-element.18) | copy-start | bytes 3317764
  146.6 6.6 %collective-permute-start = (f32[4,1,12,720]{3,1,2,0:T(1,128)S(1)}, f32[4,1,12,720]{3,1,2,0:T(1,128)S(1)}, u32[]{:S(2)}, u32[]{:S(2)}) collective-permute-start(f32[4,1,12,720]{3,1,2,0:T(1,128)S(1)} %get-tuple-element.11), channel_id=1, source_target_pairs={{0,1},{1,2},{2,3},{3,4},{4,5},{5,6},{6,7},{7,0},{8,9},{9,10},{10,1... | collective-permute-start | bytes 414728 | tf_op jit(solution)/shard_map/ppermute | solution.py:18
  146.6 6.5 %collective-permute-start.1 = (f32[4,1,12,720]{3,1,2,0:T(1,128)S(1)}, f32[4,1,12,720]{3,1,2,0:T(1,128)S(1)}, u32[]{:S(2)}, u32[]{:S(2)}) collective-permute-start(f32[4,1,12,720]{3,1,2,0:T(1,128)S(1)} %get-tuple-element.12), channel_id=1, source_target_pairs={{1,0},{2,1},{3,2},{4,3},{5,4},{6,5},{7,6},{0,7},{9,8},{10,9},{11,1... | collective-permute-start | bytes 414728 | tf_op jit(solution)/shard_map/ppermute | solution.py:19
  172.7 7.5 %collective-permute-start.2 = (f32[4,1,12,720]{3,1,2,0:T(1,128)S(1)}, f32[4,1,12,720]{3,1,2,0:T(1,128)S(1)}, u32[]{:S(2)}, u32[]{:S(2)}) collective-permute-start(f32[4,1,12,720]{3,1,2,0:T(1,128)S(1)} %get-tuple-element.9), channel_id=1, source_target_pairs={{0,1},{1,2},{2,3},{3,4},{4,5},{5,6},{6,7},{7,0},{8,9},{9,10},{10,1... | collective-permute-start | bytes 414728 | tf_op jit(solution)/shard_map/ppermute | solution.py:18
  174.0 6.3 %collective-permute-start.3 = (f32[4,1,12,720]{3,1,2,0:T(1,128)S(1)}, f32[4,1,12,720]{3,1,2,0:T(1,128)S(1)}, u32[]{:S(2)}, u32[]{:S(2)}) collective-permute-start(f32[4,1,12,720]{3,1,2,0:T(1,128)S(1)} %get-tuple-element.10), channel_id=1, source_target_pairs={{1,0},{2,1},{3,2},{4,3},{5,4},{6,5},{7,6},{0,7},{9,8},{10,9},{11,1... | collective-permute-start | bytes 414728 | tf_op jit(solution)/shard_map/ppermute | solution.py:19
Sparse Core Ops, SparseCore 0:
  10.8 57.1 all-reduce.3
  70.0 66.8 all-gather.1
where the time goes:
time: 207 us; the launch traced here: 206 us
  waiting for transfers between devices  108 us (52%)
  matrix products  29.6 us (14%)
  other arithmetic  24.1 us (12%)
  local copies, waits for them, and re-layouts  23.5 us (11%)
  between operations  13.7 us (7%)
  starting transfers between devices  7.26 us (4%)
    all_gather x1, waiting for transfers between devices, shards(): control_full = lax.all_gather(control, 'mem', axis=2, tiled=True)  66.5 us
    psum x1, waiting for transfers between devices, shards(): member_total = lax.psum(local_total, 'mem')  34.7 us
    dot_general x2, matrix products, source(): jnp.dot(field.reshape(-1, shape[-1]), kernel, precision=lax.Precision.HIG...  29.6 us
    reduce_sum x2, other arithmetic, source(): energy = jnp.mean(field * field, axis=-1, keepdims=True)  8.77 us
    mul x4, local copies, waits for them, and re-layouts, wave_tables(): alignment[..., None] * growth[None, None, None, :]  8.19 us
    mul x4, local copies, waits for them, and re-layouts, wave_tables(): cell_speed[:, :, None, :] * jnp.cos(angles)[:, None]  7.2 us
    ppermute x2, waiting for transfers between devices, extended(): before = lax.ppermute(last, axis, up)  6.83 us
    ppermute x2, starting transfers between devices, extended(): after = lax.ppermute(initial, axis, down)  5.86 us
  transfers between devices with their start and end apart: 6, of which 4 were waited for; matrix products, arithmetic and copies ran while one was open for 12% of the time, Pallas kernels for 0%

commit v1 on v0

--- a/solution.py
+++ b/solution.py
@@ -91,7 +91,16 @@
     tables = wave_tables(sea_mask, depth_class, wind_dir, growth)
     ocean = tables[3]
     member_total = lax.psum(local_total, "mem")
-    control_full = lax.all_gather(control, "mem", axis=2, tiled=True)
+    ways = lax.axis_size("mem")
+    up_2 = [(d, (d + 1) % ways) for d in range(ways)]
+    down_2 = [(d, (d - 1) % ways) for d in range(ways)]
+    earlier, later = ([control], [control])
+    for _ in range(ways // 2):
+        earlier.append(lax.ppermute(earlier[-1], "mem", up_2))
+    for _ in range((ways - 1) // 2):
+        later.append(lax.ppermute(later[-1], "mem", down_2))
+    line = jnp.concatenate([*earlier[::-1], *later[1:]], axis=2)
+    control_full = jnp.roll(line, (lax.axis_index("mem") - ways // 2) * control.shape[2], axis=2)
     field = (members - member_total / member_count + control_full) * ocean
     field = thin_step(field, tables, kernel)
     field = thin_step(field, tables, kernel)

time: 207 us -> 141 us (0.68)
  waiting for transfers between devices: 108 us -> 39.2 us
  starting transfers between devices: 7.26 us -> 12 us
    all_gather x1 -> x0, waiting for transfers between devices: 66.5 us -> none  [shards(): control_full = lax.all_gather(control, 'mem', axis=2, tiled=True)]
    psum x1, waiting for transfers between devices: 34.7 us -> 24.9 us  [shards(): member_total = lax.psum(local_total, 'mem')]
    ppermute x0 -> x3, waiting for transfers between devices: none -> 7.41 us  [the longest x2 7.41 us: shards(): earlier.append(lax.ppermute(earlier[-1], 'mem', up_2))]
    all_gather x1 -> x0, local copies, waits for them, and re-layouts: 5.41 us -> none  [shards(): control_full = lax.all_gather(control, 'mem', axis=2, tiled=True)]
    concatenate x0 -> x1, local copies, waits for them, and re-layouts: none -> 4.86 us  [shards(): jnp.roll(line, (lax.axis_index('mem') - ways // 2) * control.shape[2], ax...]
    ppermute x0 -> x3, starting transfers between devices: none -> 4.77 us  [the longest x2 3.74 us: shards(): earlier.append(lax.ppermute(earlier[-1], 'mem', up_2))]
    dynamic_slice x0 -> x1, local copies, waits for them, and re-layouts: none -> 2.76 us  [shards(): jnp.roll(line, (lax.axis_index('mem') - ways // 2) * control.shape[2], ax...]
  transfers between devices with their start and end apart: 6 -> 8, of which waited for: 4 -> 4; matrix products, arithmetic and copies ran while one was open for 12% -> 23% of each run, Pallas kernels for 0% -> 0%
where the time goes in v1:
time: 141 us
  waiting for transfers between devices  39.2 us (28%)
  matrix products  29.6 us (21%)
  local copies, waits for them, and re-layouts  23.8 us (17%)
  other arithmetic  22.7 us (16%)
  between operations  13.7 us (10%)
  starting transfers between devices  12 us (9%)
    dot_general x2, matrix products, source(): jnp.dot(field.reshape(-1, shape[-1]), kernel, precision=lax.Precision.HIG...  29.6 us
    psum x1, waiting for transfers between devices, shards(): member_total = lax.psum(local_total, 'mem')  24.9 us
    reduce_sum x2, other arithmetic, source(): energy = jnp.mean(field * field, axis=-1, keepdims=True)  8.77 us
    mul x4, local copies, waits for them, and re-layouts, wave_tables(): alignment[..., None] * growth[None, None, None, :]  8.2 us
    ppermute x2, waiting for transfers between devices, shards(): earlier.append(lax.ppermute(earlier[-1], 'mem', up_2))  7.41 us
    mul x4, local copies, waits for them, and re-layouts, wave_tables(): cell_speed[:, :, None, :] * jnp.cos(angles)[:, None]  7.21 us
    ppermute x2, waiting for transfers between devices, extended(): before = lax.ppermute(last, axis, up)  6.84 us
    ppermute x2, starting transfers between devices, extended(): after = lax.ppermute(initial, axis, down)  5.86 us
  transfers between devices with their start and end apart: 8, of which 4 were waited for; matrix products, arithmetic and copies ran while one was open for 23% of the time, Pallas kernels for 0%

profile of v1, /device:TPU:0, one launch (start us, length us, event | category | flops | bytes accessed | tf_op | source)
XLA Modules:
  0.0 141.0 jit_solution(14529423897194188133)
XLA Ops:
  6.5 0.0 copy-start.5
  6.6 0.0 all-reduce.4.cloned.1.call-start
  6.6 3.0 %collective-permute-start = (f32[32,12,180]{2,0,1:T(8,128)}, f32[32,12,180]{2,0,1:T(8,128)}, u32[]{:S(2)}, u32[]{:S(2)}) collective-permute-start(f32[32,12,180]{2,0,1:T(8,128)} %param.9), channel_id=1, source_target_pairs={{0,8},{8,16},{16,24},{24,0},{1,9},{9,17},{17,25},{25,1},{2,10},{10... | collective-permute-start | bytes 829448 | tf_op jit(solution)/shard_map/ppermute | solution.py:99
  9.6 1.0 collective-permute-start.2
  10.6 3.9 %reduce_sum.36 = f32[32,12,720]{2,0,1:T(8,128)} reduce(f32[4,32,12,720]{3,1,2,0:T(8,128)} %param.8, f32[]{:T(128)} %constant.28.clone.1), dimensions={0}, to_apply=%region_0.0 | reduce | flops 829440 | bytes 5529604 | tf_op jit(solution)/shard_map/reduce_sum | solution.py:90
  14.5 0.0 all-reduce.4.cloned.1.call-update
  14.6 0.1 broadcast_minimum_fusion
  14.6 0.6 multiply_reduce_fusion.2
  15.3 0.0 copy-done.6
  15.3 0.1 mul.264
  15.4 0.1 mul.265
  15.5 0.1 mul.256
  15.6 0.1 mul.257
  15.7 0.1 mul.275
  15.8 0.1 copy.11
  15.9 0.7 cosine_maximum_fusion
  16.7 3.2 %mul.272 = f32[32,12,24,30]{3,2,0,1:T(8,128)} broadcast(f32[32,12,24]{2,0,1:T(8,128)S(1)} %cosine_maximum_fusion), dimensions={0,1,2} | broadcast | bytes 1142784 | tf_op jit(solution)/shard_map/mul | solution.py:43
  19.9 4.9 %mul.273 = f32[32,12,720]{2,0,1:T(8,128)} reshape(f32[32,12,24,30]{3,2,0,1:T(8,128)} %mul.272) | data formatting | bytes 2211840 | tf_op jit(solution)/shard_map/mul | solution.py:43
  24.8 2.5 %mul.254 = f32[32,12,24,30]{3,2,0,1:T(8,128)} broadcast(f32[32,12,30]{2,0,1:T(8,128)S(1)} %copy.11), dimensions={0,1,3} | broadcast | bytes 1152000 | tf_op jit(solution)/shard_map/mul | solution.py:35
  27.3 4.6 %mul.255 = f32[32,12,720]{2,0,1:T(8,128)} reshape(f32[32,12,24,30]{3,2,0,1:T(8,128)} %mul.254) | data formatting | bytes 2211840 | tf_op jit(solution)/shard_map/mul | solution.py:35
  31.8 0.0 collective-permute-done
  31.8 0.8 collective-permute-start.1
  32.6 3.4 %multiply_maximum_fusion.1 = (f32[32,12,720]{2,0,1:T(8,128)S(1)}, f32[32,12,720]{2,0,1:T(8,128)}, f32[32,12,720]{2,0,1:T(8,128)}, f32[32,12,720]{2,0,1:T(8,128)}) fusion(f32[32,12,720]{2,0,1:T(8,128)} %mul.255, f32[720]{0:T(1024)S(1)} %mul.257, f32[720]{0:T(1024)S(1)} %mul.265), kind=kLoop, calls=%fused_computation.44 | loop fusion | flops 1658880 | bytes 5535360 | tf_op jit(solution)/shard_map/max | solution.py:54
  36.0 0.0 collective-permute-done.2
  36.0 7.4 %collective-permute-done.1 = f32[32,12,180]{2,0,1:T(8,128)} collective-permute-done((f32[32,12,180]{2,0,1:T(8,128)}, f32[32,12,180]{2,0,1:T(8,128)}, u32[]{:S(2)}, u32[]{:S(2)}) %collective-permute-start.1) | collective-permute-done | bytes 276512 | tf_op jit(solution)/shard_map/ppermute | solution.py:99
  43.4 4.9 %concatenate.20 = f32[32,12,1440]{2,0,1:T(8,128)} concatenate(f32[32,12,180]{2,0,1:T(8,128)} %collective-permute-done.1, f32[32,12,180]{2,0,1:T(8,128)} %collective-permute-done, f32[32,12,180]{2,0,1:T(8,128)} %param.9, f32[32,12,180]{2,0,1:T(8,128)} %collective-permute-done.2, f32[32,12,180]{2,0,1:T(8,128)} %collective-permute-done.1, f32[32,12,180]{2,0,1:T(8,128)} %collective-permute-done, ...), dimensions={2} | concatenate | bytes 4423680 | tf_op jit(solution)/shard_map/jit(_roll_dynamic)/concatenate | solution.py:103
  48.3 2.8 %constant_dynamic-slice_fusion = f32[32,12,720]{2,0,1:T(8,128)} fusion(f32[32,12,1440]{2,0,1:T(8,128)} %concatenate.20, s32[]{:T(128)S(6)} %select_n.14), kind=kLoop, calls=%fused_computation.59 | loop fusion | bytes 2211844 | tf_op jit(solution)/shard_map/jit(_roll_dynamic)/dynamic_slice | solution.py:103
  51.0 24.9 %all-reduce.4.cloned.1.call-done = f32[32,12,720]{2,0,1:T(8,128)} async-done(((f32[32,12,720]{2,0,1:T(8,128)}), f32[32,12,720]{2,0,1:T(8,128)}) %all-reduce.4.cloned.1.call-update) | async-done | bytes 1105936 | tf_op jit(solution)/shard_map/psum | solution.py:93
  75.9 1.4 broadcast_multiply_fusion.1
  77.3 0.0 copy-start.4
  77.3 0.0 copy-start.1
  77.3 0.0 copy-start.2
  77.3 3.8 %add_multiply_fusion.2 = f32[4,32,12,720]{3,1,2,0:T(8,128)S(1)} fusion(f32[4,32,12,720]{3,1,2,0:T(8,128)} %param.8, f32[32,12]{0,1:T(8,128)S(1)} %convert_element_type.39, f32[32,12,720]{2,0,1:T(8,128)} %constant_dynamic-slice_fusion, f32[32,12,720]{2,0,1:T(8,128)S(1)} %broadcast_multiply_fusion.1), kind=kLoop, calls=%fused_computation.36 | loop fusion | flops 3317760 | bytes 11060736 | tf_op jit(solution)/shard_map/mul | solution.py:104
  81.1 0.2 fusion.38
  81.3 0.1 collective-permute-start.3
  81.4 3.5 %collective-permute-start.4 = (f32[4,1,12,720]{3,1,2,0:T(1,128)S(1)}, f32[4,1,12,720]{3,1,2,0:T(1,128)S(1)}, u32[]{:S(2)}, u32[]{:S(2)}) collective-permute-start(f32[4,1,12,720]{3,1,2,0:T(1,128)S(1)} %get-tuple-element.12), channel_id=1, source_target_pairs={{1,0},{2,1},{3,2},{4,3},{5,4},{6,5},{7,6},{0,7},{9,8},{10,9},{11,1... | collective-permute-start | bytes 414728 | tf_op jit(solution)/shard_map/ppermute | solution.py:19
  84.9 0.1 broadcast_multiply_fusion
  85.0 2.9 %collective-permute-done.3 = f32[4,1,12,720]{3,1,2,0:T(1,128)S(1)} collective-permute-done((f32[4,1,12,720]{3,1,2,0:T(1,128)S(1)}, f32[4,1,12,720]{3,1,2,0:T(1,128)S(1)}, u32[]{:S(2)}, u32[]{:S(2)}) %collective-permute-start.3) | collective-permute-done | bytes 138272 | tf_op jit(solution)/shard_map/ppermute | solution.py:18
  87.9 0.0 collective-permute-done.4
  87.9 4.5 %multiply_reduce_fusion.1 = (f32[4,32,12]{1,2,0:T(8,128)S(1)}, f32[4,32,12,720]{3,1,2,0:T(8,128)S(1)}) fusion(f32[4,32,12,720]{3,1,2,0:T(8,128)S(1)} %add_multiply_fusion.2, f32[32,12,720]{2,0,1:T(8,128)S(1)} %copy-done.2, f32[32,12,720]{2,0,1:T(8,128)S(1)} %copy-done.3, f32[4,1,12,720]{3,1,2,0:T(1,128)S(1)} %collective-permute-done.4, ...), kind=kLoop, calls=%fused_computation.35 | loop fusion | flops 17693184 | bytes 13553664 | tf_op jit(solution)/shard_map/reduce_sum | solution.py:66
  92.4 14.8 %add_multiply_fusion.1 = f32[4,32,12,720]{3,1,2,0:T(8,128)S(1)} fusion(f32[4,32,12,720]{3,1,2,0:T(8,128)S(1)} %get-tuple-element.8, f32[4,32,12]{1,2,0:T(8,128)S(1)} %broadcast_multiply_fusion.4, f32[32,12,720]{2,0,1:T(8,128)S(1)} %broadcast_multiply_fusion, f32[32,12]{0,1:T(8,128)S(1)} %convert_element_type.39, f32[720,720]{1,0:T(8,128)S(1)} %copy-done), kind=kOutput, calls=%fused_computation.34 | convolution fusion | flops 9562890240 | bytes 12034560 | tf_op jit(solution)/shard_map/dot_general | solution.py:68
  107.3 0.2 fusion.37
  107.5 1.3 collective-permute-start.5
  108.7 2.3 %collective-permute-start.6 = (f32[4,1,12,720]{3,1,2,0:T(1,128)S(1)}, f32[4,1,12,720]{3,1,2,0:T(1,128)S(1)}, u32[]{:S(2)}, u32[]{:S(2)}) collective-permute-start(f32[4,1,12,720]{3,1,2,0:T(1,128)S(1)} %get-tuple-element.10), channel_id=1, source_target_pairs={{1,0},{2,1},{3,2},{4,3},{5,4},{6,5},{7,6},{0,7},{9,8},{10,9},{11,1... | collective-permute-start | bytes 414728 | tf_op jit(solution)/shard_map/ppermute | solution.py:19
  111.1 4.0 %collective-permute-done.5 = f32[4,1,12,720]{3,1,2,0:T(1,128)S(1)} collective-permute-done((f32[4,1,12,720]{3,1,2,0:T(1,128)S(1)}, f32[4,1,12,720]{3,1,2,0:T(1,128)S(1)}, u32[]{:S(2)}, u32[]{:S(2)}) %collective-permute-start.5) | collective-permute-done | bytes 138272 | tf_op jit(solution)/shard_map/ppermute | solution.py:18
  115.0 0.0 collective-permute-done.6
  115.0 4.3 %multiply_reduce_fusion = (f32[4,32,12]{1,2,0:T(8,128)S(1)}, f32[4,32,12,720]{3,1,2,0:T(8,128)S(1)}) fusion(f32[4,32,12,720]{3,1,2,0:T(8,128)S(1)} %add_multiply_fusion.1, f32[32,12,720]{2,0,1:T(8,128)S(1)} %copy-done.2, f32[32,12,720]{2,0,1:T(8,128)S(1)} %copy-done.3, f32[4,1,12,720]{3,1,2,0:T(1,128)S(1)} %collective-permute-done.6, ...), kind=kLoop, calls=%fused_computation.33 | loop fusion | flops 17693184 | bytes 13553664 | tf_op jit(solution)/shard_map/reduce_sum | solution.py:66
  119.3 14.8 %add_multiply_fusion = f32[4,32,12,720]{3,1,2,0:T(8,128)} fusion(f32[4,32,12,720]{3,1,2,0:T(8,128)S(1)} %get-tuple-element.6, f32[4,32,12]{1,2,0:T(8,128)S(1)} %broadcast_multiply_fusion.3, f32[32,12,720]{2,0,1:T(8,128)S(1)} %broadcast_multiply_fusion, f32[32,12]{0,1:T(8,128)S(1)} %convert_element_type.39, f32[720,720]{1,0:T(8,128)S(1)} %copy-done), kind=kOutput, calls=%fused_computation.32 | convolution fusion | flops 9562890240 | bytes 12034560 | tf_op jit(solution)/shard_map/dot_general | solution.py:68
  (24 shorter events, 0.2 us)
Async XLA Ops:
  6.5 85.9 %copy-start = (f32[720,720]{1,0:T(8,128)S(1)}, f32[720,720]{1,0:T(8,128)}, u32[]{:S(2)}) copy-start(f32[720,720]{1,0:T(8,128)} %param.14) | copy-start | bytes 6220804
  6.5 8.0 %copy-start.9 = (f32[4]{0:T(128)S(1)}, f32[4]{0:T(128)}, u32[]{:S(2)}) copy-start(f32[4]{0:T(128)} %constant.78) | copy-start | bytes 52
  6.5 8.0 %copy-start.7 = (s32[32,12]{0,1:T(8,128)S(1)}, s32[32,12]{0,1:T(8,128)}, u32[]{:S(2)}) copy-start(s32[32,12]{0,1:T(8,128)} %param.11) | copy-start | bytes 4612
  6.5 8.8 %copy-start.6 = (s32[32,12]{0,1:T(8,128)S(1)}, s32[32,12]{0,1:T(8,128)}, u32[]{:S(2)}) copy-start(s32[32,12]{0,1:T(8,128)} %param.10) | copy-start | bytes 4612
  6.5 9.1 %copy-start.8 = (f32[30]{0:T(128)S(1)}, f32[30]{0:T(128)}, u32[]{:S(2)}) copy-start(f32[30]{0:T(128)} %param.13) | copy-start | bytes 364
  6.5 9.4 %copy-start.5 = (s32[32,12]{0,1:T(8,128)S(1)}, s32[32,12]{0,1:T(8,128)}, u32[]{:S(2)}) copy-start(s32[32,12]{0,1:T(8,128)} %param.12) | copy-start | bytes 4612
  6.6 69.4 %all-reduce.4.cloned.1.call-start = ((), (), s32[]{:S(2)}) async-start(), calls=%async_computation | async-start | bytes 2359296 | tf_op jit(solution)/shard_map/psum | solution.py:93
  6.6 25.2 %collective-permute-start = (f32[32,12,180]{2,0,1:T(8,128)}, f32[32,12,180]{2,0,1:T(8,128)}, u32[]{:S(2)}, u32[]{:S(2)}) collective-permute-start(f32[32,12,180]{2,0,1:T(8,128)} %param.9), channel_id=1, source_target_pairs={{0,8},{8,16},{16,24},{24,0},{1,9},{9,17},{17,25},{25,1},{2,10},{10... | collective-permute-start | bytes 829448 | tf_op jit(solution)/shard_map/ppermute | solution.py:99
  9.6 26.4 %collective-permute-start.2 = (f32[32,12,180]{2,0,1:T(8,128)}, f32[32,12,180]{2,0,1:T(8,128)}, u32[]{:S(2)}, u32[]{:S(2)}) collective-permute-start(f32[32,12,180]{2,0,1:T(8,128)} %param.9), channel_id=1, source_target_pairs={{0,24},{8,0},{16,8},{24,16},{1,25},{9,1},{17,9},{25,17},{2,26},{10... | collective-permute-start | bytes 829448 | tf_op jit(solution)/shard_map/ppermute | solution.py:101
  31.8 11.6 %collective-permute-start.1 = (f32[32,12,180]{2,0,1:T(8,128)}, f32[32,12,180]{2,0,1:T(8,128)}, u32[]{:S(2)}, u32[]{:S(2)}) collective-permute-start(f32[32,12,180]{2,0,1:T(8,128)} %collective-permute-done), channel_id=1, source_target_pairs={{0,8},{8,16},{16,24},{24,0},{1,9},{9,17},{17,25},{25,1},{2,10},{10... | collective-permute-start | bytes 829448 | tf_op jit(solution)/shard_map/ppermute | solution.py:99
  77.3 7.6 %copy-start.4 = (f32[32,12,720]{2,0,1:T(8,128)S(1)}, f32[32,12,720]{2,0,1:T(8,128)}, u32[]{:S(2)}) copy-start(f32[32,12,720]{2,0,1:T(8,128)} %mul.273) | copy-start | bytes 3317764
  77.3 10.6 %copy-start.1 = (f32[32,12,720]{2,0,1:T(8,128)S(1)}, f32[32,12,720]{2,0,1:T(8,128)}, u32[]{:S(2)}) copy-start(f32[32,12,720]{2,0,1:T(8,128)} %get-tuple-element.14) | copy-start | bytes 3317764
  77.3 10.6 %copy-start.2 = (f32[32,12,720]{2,0,1:T(8,128)S(1)}, f32[32,12,720]{2,0,1:T(8,128)}, u32[]{:S(2)}) copy-start(f32[32,12,720]{2,0,1:T(8,128)} %get-tuple-element.17) | copy-start | bytes 3317764
  77.3 10.6 %copy-start.3 = (f32[32,12,720]{2,0,1:T(8,128)S(1)}, f32[32,12,720]{2,0,1:T(8,128)}, u32[]{:S(2)}) copy-start(f32[32,12,720]{2,0,1:T(8,128)} %get-tuple-element.18) | copy-start | bytes 3317764
  81.3 6.6 %collective-permute-start.3 = (f32[4,1,12,720]{3,1,2,0:T(1,128)S(1)}, f32[4,1,12,720]{3,1,2,0:T(1,128)S(1)}, u32[]{:S(2)}, u32[]{:S(2)}) collective-permute-start(f32[4,1,12,720]{3,1,2,0:T(1,128)S(1)} %get-tuple-element.11), channel_id=1, source_target_pairs={{0,1},{1,2},{2,3},{3,4},{4,5},{5,6},{6,7},{7,0},{8,9},{9,10},{10,1... | collective-permute-start | bytes 414728 | tf_op jit(solution)/shard_map/ppermute | solution.py:18
  81.4 6.5 %collective-permute-start.4 = (f32[4,1,12,720]{3,1,2,0:T(1,128)S(1)}, f32[4,1,12,720]{3,1,2,0:T(1,128)S(1)}, u32[]{:S(2)}, u32[]{:S(2)}) collective-permute-start(f32[4,1,12,720]{3,1,2,0:T(1,128)S(1)} %get-tuple-element.12), channel_id=1, source_target_pairs={{1,0},{2,1},{3,2},{4,3},{5,4},{6,5},{7,6},{0,7},{9,8},{10,9},{11,1... | collective-permute-start | bytes 414728 | tf_op jit(solution)/shard_map/ppermute | solution.py:19
  107.5 7.6 %collective-permute-start.5 = (f32[4,1,12,720]{3,1,2,0:T(1,128)S(1)}, f32[4,1,12,720]{3,1,2,0:T(1,128)S(1)}, u32[]{:S(2)}, u32[]{:S(2)}) collective-permute-start(f32[4,1,12,720]{3,1,2,0:T(1,128)S(1)} %get-tuple-element.9), channel_id=1, source_target_pairs={{0,1},{1,2},{2,3},{3,4},{4,5},{5,6},{6,7},{7,0},{8,9},{9,10},{10,1... | collective-permute-start | bytes 414728 | tf_op jit(solution)/shard_map/ppermute | solution.py:18
  108.7 6.3 %collective-permute-start.6 = (f32[4,1,12,720]{3,1,2,0:T(1,128)S(1)}, f32[4,1,12,720]{3,1,2,0:T(1,128)S(1)}, u32[]{:S(2)}, u32[]{:S(2)}) collective-permute-start(f32[4,1,12,720]{3,1,2,0:T(1,128)S(1)} %get-tuple-element.10), channel_id=1, source_target_pairs={{1,0},{2,1},{3,2},{4,3},{5,4},{6,5},{7,6},{0,7},{9,8},{10,9},{11,1... | collective-permute-start | bytes 414728 | tf_op jit(solution)/shard_map/ppermute | solution.py:19
Sparse Core Ops, SparseCore 0:
  14.6 61.2 all-reduce.3
